TPU v7x, 32 devices: a whole 2x2x4 slice. The times are simulated.
32 devices in a mesh: rad: 4 (over y, core), azi: 8 (over z, x).
Axes of the slice: x: 2, y: 2, z: 4, core: 2. Of those that a mesh axis runs over, the one named last changes fastest.
Arguments:
- fields: float32 [5, 8, 512, 512], P(None, None, 'azi', 'rad'), may hold values from -6 to 6
- radial_metric: float32 [512], P('rad'), may hold values from 0.5 to 2
- azimuth_metric: float32 [512], P('rad'), may hold values from 0.5 to 2
Outputs:
- grad_azimuth: float32 [5, 8, 512, 512], P(None, None, 'azi', 'rad')
- grad_radial: float32 [5, 8, 512, 512], P(None, None, 'azi', 'rad')
- filtered: float32 [5, 8, 512, 512], P(None, None, 'azi', 'rad')
All inputs are finite; a program needn't handle non-finite values.
Results may differ from a plain program's by a relative error of at most 0.0003.
Values sent between devices are 32-bit elements; how exact they have to be, the bound alone decides.
A program may use at most 192 MiB of HBM per device.

v0:
```python
import functools

import jax
import jax.numpy as jnp
import ml_dtypes
import numpy as np
from jax import lax
from jax.experimental import pallas as pl
from jax.experimental.pallas import tpu as pltpu
from jax.sharding import PartitionSpec as P

ALPHA_D = 1.0 / 3.0
COEF_A = 14.0 / 9.0
COEF_B = 1.0 / 9.0
ALPHA_F = 0.49
MESH = pl.DeviceIdType.MESH
BF16 = jnp.bfloat16
F32 = jnp.float32

EDGE = 6
PACK = 4


def filter_weights():
    slack = 1.0 - 2.0 * ALPHA_F
    return [
        (193.0 + 126.0 * ALPHA_F) / 256.0,
        (105.0 + 302.0 * ALPHA_F) / 256.0,
        -15.0 * slack / 64.0,
        45.0 * slack / 512.0,
        -5.0 * slack / 256.0,
        slack / 512.0,
    ]


def split(table):
    table = np.asarray(table, np.float32)
    high = table.astype(ml_dtypes.bfloat16)
    low = (table - high.astype(np.float32)).astype(ml_dtypes.bfloat16)
    return high, low


def decay(alpha):
    return (-1.0 + np.sqrt(1.0 - 4.0 * alpha * alpha)) / (2.0 * alpha)


def azimuth_tables(cells, blocks):
    total = cells * blocks
    wave = 2.0 * np.pi * np.arange(total) / total
    slope_symbol = 1j * (COEF_A * np.sin(wave) + 0.5 * COEF_B * np.sin(2.0 * wave))
    slope_symbol = slope_symbol / (1.0 + 2.0 * ALPHA_D * np.cos(wave))
    weights = filter_weights()
    smooth_symbol = sum(w * np.cos(n * wave) for n, w in enumerate(weights))
    smooth_symbol = smooth_symbol / (1.0 + 2.0 * ALPHA_F * np.cos(wave))
    slope = np.real(np.fft.ifft(slope_symbol))
    smooth = np.real(np.fft.ifft(smooth_symbol))
    i = np.arange(cells)
    gap = (i[:, None] - i[None, :]) % total
    main = np.concatenate([slope[gap], smooth[gap]], axis=0)
    rate_d, rate_f = decay(ALPHA_D), decay(ALPHA_F)
    scale_d = slope[2] / rate_d**2
    scale_f = smooth[5] / rate_f**5
    send_right = np.zeros((EDGE, cells))
    send_right[0] = rate_d ** (cells - 1 - i)
    send_right[1] = rate_f ** (cells - 1 - i)
    use_left = np.zeros((2 * cells, EDGE))
    use_left[:cells, 0] = scale_d * rate_d ** (i + 1)
    use_left[cells:, 1] = scale_f * rate_f ** (i + 1)
    for m in range(EDGE - 2):
        send_right[2 + m, cells - 1 - m] = 1.0
        for row in range(EDGE - 2 - m):
            n = row + 1 + m
            if n < 2:
                use_left[row, 2 + m] = slope[n] - scale_d * rate_d**n
            if n < 5:
                use_left[cells + row, 2 + m] = smooth[n] - scale_f * rate_f**n
    send_left = send_right[:, ::-1]
    use_right = np.concatenate([-use_left[:cells][::-1], use_left[cells:][::-1]], axis=0)
    return main, send_right, send_left, use_left, use_right


def radial_matrix(total):
    system = np.eye(total) + ALPHA_D * (np.eye(total, k=1) + np.eye(total, k=-1))
    side = 0.5 * COEF_A * (np.eye(total, k=1) - np.eye(total, k=-1))
    side = side + 0.25 * COEF_B * (np.eye(total, k=2) - np.eye(total, k=-2))
    return np.linalg.solve(system, side)


def rank_two(corner):
    cells = corner.shape[0]
    send = np.zeros((2, cells))
    send[0] = corner[1] / corner[1, cells - 1]
    send[1, cells - 1] = 1.0
    use = np.zeros((cells, 2))
    use[1:, 0] = corner[1:, cells - 1]
    use[0, 0] = corner[0, cells - 2] / send[0, cells - 2]
    use[0, 1] = corner[0, cells - 1] - use[0, 0]
    return use, send


def radial_tables(cells, blocks):
    full = radial_matrix(cells * blocks).reshape(blocks, cells, blocks, cells)
    main = np.stack([full[b, :, b, :] for b in range(blocks)])
    use_left = np.zeros((blocks, cells, 2))
    use_right = np.zeros((blocks, cells, 2))
    send_right = np.zeros((blocks, 2, cells))
    send_left = np.zeros((blocks, 2, cells))
    for b in range(1, blocks):
        use_left[b], send_right[b - 1] = rank_two(full[b, :, b - 1, :])
    for b in range(blocks - 1):
        use, send = rank_two(full[b, :, b + 1, :][::-1, ::-1])
        use_right[b], send_left[b + 1] = use[::-1], send[:, ::-1]
    return main, send_right, send_left, use_left, use_right


def build_tables(cells_t, azi_count, cells_r, rad_count):
    main, send_right, send_left, use_left, use_right = azimuth_tables(cells_t, azi_count)
    sends = np.zeros((16, cells_t))
    sends[:EDGE], sends[8 : 8 + EDGE] = send_right, send_left
    high, low = split(sends)
    azi_send = np.concatenate([high, low, high], axis=1)
    uses = np.zeros((2 * cells_t, 16))
    uses[:, :EDGE], uses[:, 8 : 8 + EDGE] = use_left, use_right
    high, low = split(main)
    use_high, use_low = split(uses)
    azi_main = np.concatenate([high, low, high], axis=1)
    azi_use = np.concatenate([use_high, use_low, use_high], axis=1)

    main, send_right, send_left, use_left, use_right = radial_tables(cells_r, rad_count)
    sends = np.concatenate([send_right, send_left], axis=1)
    high, low = split(sends)
    rad_send = np.zeros((rad_count, 16, 2 * cells_r), ml_dtypes.bfloat16)
    rad_send[:, 0:4, :cells_r] = high
    rad_send[:, 0:4, cells_r:] = high
    rad_send[:, 8:12, :cells_r] = low
    turned = np.swapaxes(main, 1, 2)
    high, low = split(turned)
    rad_main = np.zeros((rad_count, 2 * cells_r, 2 * cells_r), ml_dtypes.bfloat16)
    rad_main[:, :cells_r, :cells_r] = high
    rad_main[:, :cells_r, cells_r:] = low
    rad_main[:, cells_r:, :cells_r] = high
    uses = np.swapaxes(np.concatenate([use_left, use_right], axis=2), 1, 2)
    high, low = split(uses)
    rad_use = np.zeros((rad_count, 16, cells_r), ml_dtypes.bfloat16)
    rad_use[:, 0:4], rad_use[:, 4:8], rad_use[:, 8:12] = high, low, high
    return azi_send, azi_main, azi_use, rad_send, rad_main, rad_use


def halves(x):
    high = x.astype(BF16)
    return high, (x - high.astype(F32)).astype(BF16)


def dot(a, b):
    return jnp.dot(a, b, preferred_element_type=F32)


def block_kernel(
    azi_count, rad_count, chunk,
    fields, azi_send, azi_main, rad_send, rad_main, rad_use, radial_metric,
    from_left, from_right, part_slope, part_smooth, grad_radial,
    block, azi_send_v, azi_main_v, rad_send_v, rad_main_v, rad_use_v, metric,
    to_right, to_left, to_out, to_in, from_in, from_out, ends,
    table_sem, load_sem, send_sem, recv_sem, rad_send_sem, rad_recv_sem,
):
    planes, cells_t, cells_r = block.shape
    count = planes // chunk
    rows = chunk * cells_t
    groups = chunk // PACK
    rad, azi = lax.axis_index("rad"), lax.axis_index("azi")
    right = (rad, lax.rem(azi + 1, azi_count))
    left = (rad, lax.rem(azi + azi_count - 1, azi_count))
    outer = (lax.rem(rad + 1, rad_count), azi)
    inner = (lax.rem(rad + rad_count - 1, rad_count), azi)
    barrier = pltpu.get_barrier_semaphore()
    for place in (right, left, outer, inner):
        pl.semaphore_signal(barrier, inc=1, device_id=place, device_id_type=MESH)

    def load(c):
        span = pl.ds(c * chunk, chunk)
        return pltpu.make_async_copy(fields.at[span], block.at[span], load_sem.at[c])

    tables = [
        pltpu.make_async_copy(source, target, table_sem.at[k])
        for k, (source, target) in enumerate(
            (
                (azi_send, azi_send_v),
                (rad_send.at[rad], rad_send_v),
                (azi_main, azi_main_v),
                (rad_main.at[rad], rad_main_v),
                (rad_use.at[rad], rad_use_v),
                (radial_metric, metric),
            )
        )
    ]
    tables[0].start()
    tables[1].start()
    for c in range(count):
        load(c).start()
    for table in tables[2:]:
        table.start()
    tables[0].wait()
    tables[1].wait()

    cuts = [0, count]

    def sends(part):
        span = pl.ds(cuts[part] * groups, (cuts[part + 1] - cuts[part]) * groups)
        return [
            pltpu.make_async_remote_copy(
                src_ref=source.at[span],
                dst_ref=target.at[span],
                send_sem=send_sem.at[k, part],
                recv_sem=recv_sem.at[k, part],
                device_id=place,
                device_id_type=MESH,
            )
            for k, (source, target, place) in enumerate(
                ((to_right, from_left, right), (to_left, from_right, left))
            )
        ]

    def edges(c):
        load(c).wait()
        high, low = halves(block[pl.ds(c * chunk, chunk)])
        for p in range(0, chunk, 2):
            edge = dot(azi_send_v[...], stacked(high, low, p))
            for k in range(2):
                group, slot = divmod(p + k, PACK)
                lanes = slice(k * cells_r, (k + 1) * cells_r)
                span = slice(EDGE * slot, EDGE * (slot + 1))
                to_right[c * groups + group, span, :] = edge[0:EDGE, lanes]
                to_left[c * groups + group, span, :] = edge[8 : 8 + EDGE, lanes]

    def radial_edges(c):
        high, low = halves(block[pl.ds(c * chunk, chunk)])
        tips = lax.dot_general(
            rad_send_v[...], paired(high, low), (((1,), (1,)), ((), ())),
            preferred_element_type=F32,
        )
        tips = tips[0:8] + tips[8:16]
        span = pl.ds(pl.multiple_of(c * rows, rows), rows)
        to_out[:, span] = tips[0:2]
        to_in[:, span] = tips[2:4]

    azimuth_copies = []
    for part in range(len(cuts) - 1):
        pl.loop(cuts[part], cuts[part + 1])(edges)
        if part == 0:
            pl.semaphore_wait(barrier, 4)
        for copy in sends(part):
            copy.start()
            azimuth_copies.append(copy)

    @pl.loop(0, count)
    def _(c):
        radial_edges(c)

    radial_copies = [
        pltpu.make_async_remote_copy(
            src_ref=source,
            dst_ref=target,
            send_sem=rad_send_sem.at[k],
            recv_sem=rad_recv_sem.at[k],
            device_id=place,
            device_id_type=MESH,
        )
        for k, (source, target, place) in enumerate(
            ((to_out, from_in, outer), (to_in, from_out, inner))
        )
    ]
    for copy in radial_copies:
        copy.start()
    for table in tables[2:]:
        table.wait()
    ends[...] = jnp.zeros_like(ends)

    @pl.loop(0, count)
    def _(c):
        high, low = halves(block[pl.ds(c * chunk, chunk)])
        for p in range(0, chunk, 2):
            result = dot(azi_main_v[...], stacked(high, low, p))
            for k in range(2):
                lanes = slice(k * cells_r, (k + 1) * cells_r)
                part_slope[c * chunk + p + k] = result[:cells_t, lanes]
                part_smooth[c * chunk + p + k] = result[cells_t:, lanes]

    for copy in radial_copies:
        copy.wait()

    @pl.loop(0, count)
    def _(c):
        span = pl.ds(pl.multiple_of(c * rows, rows), rows)
        ends[0:2] = from_in[:, span]
        ends[2:4] = from_out[:, span]
        rim = ends[0:4]
        rim_high = rim.astype(BF16).astype(F32)
        ends[0:4] = rim_high
        ends[4:8] = rim_high
        ends[8:12] = rim - rim_high
        high, low = halves(block[pl.ds(c * chunk, chunk)])
        both = dot(paired(high, low), rad_main_v[...])
        outside = lax.dot_general(
            ends[...].astype(BF16), rad_use_v[...], (((0,), (0,)), ((), ())),
            preferred_element_type=F32,
        )
        slope = (both[:, :cells_r] + both[:, cells_r:] + outside) * metric[...]
        grad_radial[pl.ds(c * chunk, chunk)] = slope.reshape(chunk, cells_t, cells_r)

    for copy in azimuth_copies:
        copy.wait()


def stacked(high, low, p):
    return jnp.concatenate(
        [jnp.concatenate([high[q], high[q], low[q]], axis=0) for q in (p, p + 1)], axis=1
    )


def paired(high, low):
    planes, cells_t, cells_r = high.shape
    rows = planes * cells_t
    return jnp.concatenate([high.reshape(rows, cells_r), low.reshape(rows, cells_r)], axis=1)


def join_kernel(
    chunk, part_slope, part_smooth, radial, from_left, from_right, azi_use, azimuth_metric,
    grad_azimuth, filtered, grad_radial,
    slopes, smooths, rims, radial_sem, sems,
):
    planes, cells_t, cells_r = part_slope.shape
    count = planes // chunk
    groups = chunk // PACK
    radial_copy = pltpu.make_async_copy(radial, grad_radial, radial_sem)
    radial_copy.start()
    rims[...] = jnp.zeros_like(rims)

    def stores(c):
        span = pl.ds(c * chunk, chunk)
        return [
            pltpu.make_async_copy(source.at[span], target.at[span], sems.at[k, c])
            for k, (source, target) in enumerate(((slopes, grad_azimuth), (smooths, filtered)))
        ]

    @pl.loop(0, count)
    def _(c):
        for p in range(chunk):
            group, slot = divmod(p, PACK)
            span = slice(EDGE * slot, EDGE * (slot + 1))
            rims[p, 0:EDGE, :] = from_left[c * groups + group, span, :]
            rims[p, 8 : 8 + EDGE, :] = from_right[c * groups + group, span, :]
        high, low = halves(rims[...])
        for p in range(0, chunk, 2):
            result = dot(azi_use[...], stacked(high, low, p))
            for k in range(2):
                q = c * chunk + p + k
                lanes = slice(k * cells_r, (k + 1) * cells_r)
                slopes[q] = (part_slope[q] + result[:cells_t, lanes]) * azimuth_metric[...]
                smooths[q] = part_smooth[q] + result[cells_t:, lanes]
        for copy in stores(c):
            copy.start()

    @pl.loop(0, count)
    def _(c):
        for copy in stores(c):
            copy.wait()

    radial_copy.wait()


def local(tables, azi_count, rad_count, fields, radial_metric, azimuth_metric):
    azi_send, azi_main, azi_use, rad_send, rad_main, rad_use = [jnp.asarray(t) for t in tables]
    shape = fields.shape
    cells_t, cells_r = shape[2], shape[3]
    planes = shape[0] * shape[1]
    x = fields.reshape(planes, cells_t, cells_r)
    chunk = 8
    count = planes // chunk
    rims = jax.ShapeDtypeStruct((planes // PACK, PACK * EDGE, cells_r), F32)
    full = jax.ShapeDtypeStruct(x.shape, F32)
    ends = pltpu.VMEM((2, planes * cells_t), F32)
    hbm = pl.BlockSpec(memory_space=pltpu.HBM)
    vmem = pl.BlockSpec(memory_space=pltpu.VMEM)
    dma = pltpu.SemaphoreType.DMA
    from_left, from_right, part_slope, part_smooth, radial = pl.pallas_call(
        functools.partial(block_kernel, azi_count, rad_count, chunk),
        out_shape=[rims, rims, full, full, full],
        in_specs=[hbm] * 7,
        out_specs=[vmem] * 5,
        scratch_shapes=[
            pltpu.VMEM(x.shape, F32),
            pltpu.VMEM(azi_send.shape, BF16),
            pltpu.VMEM(azi_main.shape, BF16),
            pltpu.VMEM(rad_send.shape[1:], BF16),
            pltpu.VMEM(rad_main.shape[1:], BF16),
            pltpu.VMEM(rad_use.shape[1:], BF16),
            pltpu.VMEM((1, cells_r), F32),
            pltpu.VMEM(rims.shape, F32),
            pltpu.VMEM(rims.shape, F32),
            ends,
            ends,
            ends,
            ends,
            pltpu.VMEM((16, chunk * cells_t), F32),
            dma((6,)),
            dma((count,)),
            dma((2, 1)),
            dma((2, 1)),
            dma((2,)),
            dma((2,)),
        ],
        compiler_params=pltpu.CompilerParams(
            collective_id=0, has_side_effects=True, vmem_limit_bytes=24 * 2**20
        ),
    )(
        *[
            pltpu.with_memory_space_constraint(a, pltpu.HBM)
            for a in (x, azi_send, azi_main, rad_send, rad_main, rad_use, radial_metric.reshape(1, cells_r))
        ]
    )

    outs = pl.pallas_call(
        functools.partial(join_kernel, chunk),
        out_shape=[full] * 3,
        in_specs=[vmem] * 7,
        out_specs=[hbm] * 3,
        scratch_shapes=[
            pltpu.VMEM(x.shape, F32),
            pltpu.VMEM(x.shape, F32),
            pltpu.VMEM((chunk, 16, cells_r), F32),
            dma,
            dma((2, count)),
        ],
        compiler_params=pltpu.CompilerParams(vmem_limit_bytes=24 * 2**20),
    )(
        part_slope, part_smooth, radial, from_left, from_right, azi_use,
        azimuth_metric.reshape(1, cells_r),
    )
    grad_azimuth, filtered, grad_radial = [a.reshape(shape) for a in outs]
    return grad_azimuth, grad_radial, filtered


def solution(mesh):
    rad_count, azi_count = mesh.shape["rad"], mesh.shape["azi"]
    spec = P(None, None, "azi", "rad")

    def run(fields, radial_metric, azimuth_metric):
        tables = build_tables(
            fields.shape[2] // azi_count, azi_count, fields.shape[3] // rad_count, rad_count
        )
        body = functools.partial(local, tables, azi_count, rad_count)
        return jax.shard_map(
            body,
            mesh=mesh,
            in_specs=(spec, P("rad"), P("rad")),
            out_specs=(spec, spec, spec),
            check_vma=False,
        )(fields, radial_metric, azimuth_metric)

    return run
```

profile of v0, /device:TPU:1, one launch (start us, length us, event | category | flops | bytes accessed | tf_op | source)
XLA Modules:
  0.0 14.2 jit_solution(8247700723147630632)
XLA Ops:
  0.6 0.0 copy-start
  0.6 0.0 copy-start.1
  0.7 11.5 %shard_map.112 = (f32[10,24,128]{2,1,0:T(8,128)S(1)}, f32[10,24,128]{2,1,0:T(8,128)S(1)}, f32[40,64,128]{2,1,0:T(8,128)S(1)}, f32[40,64,128]{2,1,0:T(8,128)S(1)}, f32[40,64,128]{2,1,0:T(8,128)S(1)}) custom-call(f32[40,64,128]{2,1,0:T(8,128)} %bitcast.7, bf16[16,192]{1,0:T(8,128)(2,1)} %constant.12.clone.azi_send, bf16[128,192]{1,0:T(8,128)(2,1)} %constant.13.clone.azi_main, ...), custom_call_target="tpu_custom_call" | custom-call | tf_op jit(solution)/shard_map/pallas_call | solution.py:385
  12.2 0.0 copy-done
  12.2 0.0 copy-done.1
  12.2 2.0 %shard_map.113 = (f32[40,64,128]{2,1,0:T(8,128)}, f32[40,64,128]{2,1,0:T(8,128)}, f32[40,64,128]{2,1,0:T(8,128)}) custom-call(f32[40,64,128]{2,1,0:T(8,128)S(1)} %get-tuple-element.11.part_slope, f32[40,64,128]{2,1,0:T(8,128)S(1)} %get-tuple-element.12.part_smooth, f32[40,64,128]{2,1,0:T(8,128)S(1)} %get-tuple-element.13.radial, ...), custom_call_target="tpu_custom_call" | custom-call | tf_op jit(solution)/shard_map/pallas_call | solution.py:422
Async XLA Ops:
  0.6 11.6 %copy-start = (bf16[128,48]{1,0:T(8,128)(2,1)S(1)}, bf16[128,48]{1,0:T(8,128)(2,1)}, u32[]{:S(2)}) copy-start(bf16[128,48]{1,0:T(8,128)(2,1)} %constant.14.clone.azi_use) | copy-start | bytes 36868
  0.6 11.6 %copy-start.1 = (f32[128]{0:T(128)S(1)}, f32[128]{0:T(128)}, u32[]{:S(2)}) copy-start(f32[128]{0:T(128)} %param.11) | copy-start | bytes 1540
where the time goes:
time: 14.4 us; the launch traced here: 14.2 us
  Pallas kernels  13.5 us (94%)
  between operations  0.67 us (5%)
    pallas_call x1, Pallas kernels, local(): pl.pallas_call(functools.partial(block_kernel, azi_count, rad_count, chun...  11.5 us
    pallas_call x1, Pallas kernels, local(): pl.pallas_call(functools.partial(join_kernel, chunk), out_shape=[full] *...  2.01 us

commit v1 on v0

--- a/solution.py
+++ b/solution.py
@@ -17,7 +17,8 @@
 BF16 = jnp.bfloat16
 F32 = jnp.float32
 
-EDGE = 6
+RAW = 4
+SUMS = 2
 PACK = 4
 
 
@@ -60,23 +61,25 @@
     rate_d, rate_f = decay(ALPHA_D), decay(ALPHA_F)
     scale_d = slope[2] / rate_d**2
     scale_f = smooth[5] / rate_f**5
-    send_right = np.zeros((EDGE, cells))
-    send_right[0] = rate_d ** (cells - 1 - i)
-    send_right[1] = rate_f ** (cells - 1 - i)
-    use_left = np.zeros((2 * cells, EDGE))
-    use_left[:cells, 0] = scale_d * rate_d ** (i + 1)
-    use_left[cells:, 1] = scale_f * rate_f ** (i + 1)
-    for m in range(EDGE - 2):
-        send_right[2 + m, cells - 1 - m] = 1.0
-        for row in range(EDGE - 2 - m):
+    send_right = np.stack([rate_d ** (cells - 1 - i), rate_f ** (cells - 1 - i)])
+    sums = np.zeros((2 * cells, SUMS))
+    sums[:cells, 0] = scale_d * rate_d ** (i + 1)
+    sums[cells:, 1] = scale_f * rate_f ** (i + 1)
+    raw = np.zeros((2 * cells, RAW))
+    for m in range(RAW):
+        for row in range(RAW - m):
             n = row + 1 + m
             if n < 2:
-                use_left[row, 2 + m] = slope[n] - scale_d * rate_d**n
+                raw[row, RAW - 1 - m] = slope[n] - scale_d * rate_d**n
             if n < 5:
-                use_left[cells + row, 2 + m] = smooth[n] - scale_f * rate_f**n
+                raw[cells + row, RAW - 1 - m] = smooth[n] - scale_f * rate_f**n
     send_left = send_right[:, ::-1]
-    use_right = np.concatenate([-use_left[:cells][::-1], use_left[cells:][::-1]], axis=0)
-    return main, send_right, send_left, use_left, use_right
+
+    def mirrored(table):
+        return np.concatenate([-table[:cells][::-1], table[cells:][::-1]], axis=0)
+
+    uses = np.concatenate([raw, mirrored(raw)[:, ::-1], sums, mirrored(sums)], axis=1)
+    return main, np.concatenate([send_right, send_left], axis=0), uses
 
 
 def radial_matrix(total):
@@ -114,13 +117,13 @@
 
 
 def build_tables(cells_t, azi_count, cells_r, rad_count):
-    main, send_right, send_left, use_left, use_right = azimuth_tables(cells_t, azi_count)
+    main, edge_sums, edge_uses = azimuth_tables(cells_t, azi_count)
     sends = np.zeros((16, cells_t))
-    sends[:EDGE], sends[8 : 8 + EDGE] = send_right, send_left
+    sends[: 2 * SUMS] = edge_sums
     high, low = split(sends)
     azi_send = np.concatenate([high, low, high], axis=1)
     uses = np.zeros((2 * cells_t, 16))
-    uses[:, :EDGE], uses[:, 8 : 8 + EDGE] = use_left, use_right
+    uses[:, : edge_uses.shape[1]] = edge_uses
     high, low = split(main)
     use_high, use_low = split(uses)
     azi_main = np.concatenate([high, low, high], axis=1)
@@ -158,10 +161,10 @@
 def block_kernel(
     azi_count, rad_count, chunk,
     fields, azi_send, azi_main, rad_send, rad_main, rad_use, radial_metric,
-    from_left, from_right, part_slope, part_smooth, grad_radial,
+    raw_left, raw_right, sum_left, sum_right, part_slope, part_smooth, grad_radial,
     block, azi_send_v, azi_main_v, rad_send_v, rad_main_v, rad_use_v, metric,
     to_right, to_left, to_out, to_in, from_in, from_out, ends,
-    table_sem, load_sem, send_sem, recv_sem, rad_send_sem, rad_recv_sem,
+    table_sem, load_sem, send_sem, recv_sem, rad_send_sem, rad_recv_sem, ready,
 ):
     planes, cells_t, cells_r = block.shape
     count = planes // chunk
@@ -172,9 +175,13 @@
     left = (rad, lax.rem(azi + azi_count - 1, azi_count))
     outer = (lax.rem(rad + 1, rad_count), azi)
     inner = (lax.rem(rad + rad_count - 1, rad_count), azi)
+    has_outer, has_inner = rad < rad_count - 1, rad > 0
     barrier = pltpu.get_barrier_semaphore()
-    for place in (right, left, outer, inner):
-        pl.semaphore_signal(barrier, inc=1, device_id=place, device_id_type=MESH)
+    pl.semaphore_signal(barrier, inc=1, device_id=left, device_id_type=MESH)
+
+    @pl.when(has_outer)
+    def _():
+        pl.semaphore_signal(barrier, inc=1, device_id=outer, device_id_type=MESH)
 
     def load(c):
         span = pl.ds(c * chunk, chunk)
@@ -193,34 +200,54 @@
             )
         )
     ]
+
+    def send(k, source, target, place):
+        return pltpu.make_async_remote_copy(
+            src_ref=source,
+            dst_ref=target,
+            send_sem=send_sem.at[k],
+            recv_sem=recv_sem.at[k],
+            device_id=place,
+            device_id_type=MESH,
+        )
+
+    raw_sends = (
+        send(0, fields.at[:, pl.ds(cells_t - RAW, RAW)], raw_left, right),
+        send(1, fields.at[:, pl.ds(0, RAW)], raw_right, left),
+    )
+    sum_sends = (send(2, to_right, sum_left, right), send(3, to_left, sum_right, left))
+    out_send, in_send = [
+        pltpu.make_async_remote_copy(
+            src_ref=source,
+            dst_ref=target,
+            send_sem=rad_send_sem.at[k],
+            recv_sem=rad_recv_sem.at[k],
+            device_id=place,
+            device_id_type=MESH,
+        )
+        for k, (source, target, place) in enumerate(
+            ((to_out, from_in, outer), (to_in, from_out, inner))
+        )
+    ]
+
     tables[0].start()
-    tables[1].start()
     for c in range(count):
         load(c).start()
-    for table in tables[2:]:
+    for table in tables[1:]:
         table.start()
+
+    pl.semaphore_wait(barrier, 1 + has_inner.astype(jnp.int32))
+    raw_sends[0].start()
+    pl.semaphore_signal(ready.at[0], inc=1, device_id=right, device_id_type=MESH)
+
+    @pl.when(has_inner)
+    def _():
+        pl.semaphore_signal(ready.at[1], inc=1, device_id=inner, device_id_type=MESH)
+
     tables[0].wait()
-    tables[1].wait()
-
-    cuts = [0, count]
-
-    def sends(part):
-        span = pl.ds(cuts[part] * groups, (cuts[part + 1] - cuts[part]) * groups)
-        return [
-            pltpu.make_async_remote_copy(
-                src_ref=source.at[span],
-                dst_ref=target.at[span],
-                send_sem=send_sem.at[k, part],
-                recv_sem=recv_sem.at[k, part],
-                device_id=place,
-                device_id_type=MESH,
-            )
-            for k, (source, target, place) in enumerate(
-                ((to_right, from_left, right), (to_left, from_right, left))
-            )
-        ]
-
-    def edges(c):
+
+    @pl.loop(0, count)
+    def _(c):
         load(c).wait()
         high, low = halves(block[pl.ds(c * chunk, chunk)])
         for p in range(0, chunk, 2):
@@ -228,11 +255,15 @@
             for k in range(2):
                 group, slot = divmod(p + k, PACK)
                 lanes = slice(k * cells_r, (k + 1) * cells_r)
-                span = slice(EDGE * slot, EDGE * (slot + 1))
-                to_right[c * groups + group, span, :] = edge[0:EDGE, lanes]
-                to_left[c * groups + group, span, :] = edge[8 : 8 + EDGE, lanes]
-
-    def radial_edges(c):
+                span = slice(SUMS * slot, SUMS * (slot + 1))
+                to_right[c * groups + group, span, :] = edge[0:SUMS, lanes]
+                to_left[c * groups + group, span, :] = edge[SUMS : 2 * SUMS, lanes]
+
+    sum_sends[0].start()
+    tables[1].wait()
+
+    @pl.loop(0, count)
+    def _(c):
         high, low = halves(block[pl.ds(c * chunk, chunk)])
         tips = lax.dot_general(
             rad_send_v[...], paired(high, low), (((1,), (1,)), ((), ())),
@@ -243,34 +274,18 @@
         to_out[:, span] = tips[0:2]
         to_in[:, span] = tips[2:4]
 
-    azimuth_copies = []
-    for part in range(len(cuts) - 1):
-        pl.loop(cuts[part], cuts[part + 1])(edges)
-        if part == 0:
-            pl.semaphore_wait(barrier, 4)
-        for copy in sends(part):
-            copy.start()
-            azimuth_copies.append(copy)
-
-    @pl.loop(0, count)
-    def _(c):
-        radial_edges(c)
-
-    radial_copies = [
-        pltpu.make_async_remote_copy(
-            src_ref=source,
-            dst_ref=target,
-            send_sem=rad_send_sem.at[k],
-            recv_sem=rad_recv_sem.at[k],
-            device_id=place,
-            device_id_type=MESH,
-        )
-        for k, (source, target, place) in enumerate(
-            ((to_out, from_in, outer), (to_in, from_out, inner))
-        )
-    ]
-    for copy in radial_copies:
-        copy.start()
+    @pl.when(has_inner)
+    def _():
+        in_send.start()
+
+    @pl.when(has_outer)
+    def _():
+        pl.semaphore_wait(ready.at[1], 1)
+        out_send.start()
+
+    pl.semaphore_wait(ready.at[0], 1)
+    raw_sends[1].start()
+    sum_sends[1].start()
     for table in tables[2:]:
         table.wait()
     ends[...] = jnp.zeros_like(ends)
@@ -285,8 +300,23 @@
                 part_slope[c * chunk + p + k] = result[:cells_t, lanes]
                 part_smooth[c * chunk + p + k] = result[cells_t:, lanes]
 
-    for copy in radial_copies:
-        copy.wait()
+    @pl.when(has_inner)
+    def _():
+        in_send.wait_send()
+        out_send.wait_recv()
+
+    @pl.when(jnp.logical_not(has_inner))
+    def _():
+        from_in[...] = jnp.zeros_like(from_in)
+
+    @pl.when(has_outer)
+    def _():
+        out_send.wait_send()
+        in_send.wait_recv()
+
+    @pl.when(jnp.logical_not(has_outer))
+    def _():
+        from_out[...] = jnp.zeros_like(from_out)
 
     @pl.loop(0, count)
     def _(c):
@@ -307,7 +337,7 @@
         slope = (both[:, :cells_r] + both[:, cells_r:] + outside) * metric[...]
         grad_radial[pl.ds(c * chunk, chunk)] = slope.reshape(chunk, cells_t, cells_r)
 
-    for copy in azimuth_copies:
+    for copy in raw_sends + sum_sends:
         copy.wait()
 
 
@@ -324,7 +354,8 @@
 
 
 def join_kernel(
-    chunk, part_slope, part_smooth, radial, from_left, from_right, azi_use, azimuth_metric,
+    chunk, part_slope, part_smooth, radial, raw_left, raw_right, sum_left, sum_right,
+    azi_use, azimuth_metric,
     grad_azimuth, filtered, grad_radial,
     slopes, smooths, rims, radial_sem, sems,
 ):
@@ -346,9 +377,11 @@
     def _(c):
         for p in range(chunk):
             group, slot = divmod(p, PACK)
-            span = slice(EDGE * slot, EDGE * (slot + 1))
-            rims[p, 0:EDGE, :] = from_left[c * groups + group, span, :]
-            rims[p, 8 : 8 + EDGE, :] = from_right[c * groups + group, span, :]
+            span = slice(SUMS * slot, SUMS * (slot + 1))
+            rims[p, 0:RAW, :] = raw_left[c * chunk + p]
+            rims[p, RAW : 2 * RAW, :] = raw_right[c * chunk + p]
+            rims[p, 8:10, :] = sum_left[c * groups + group, span, :]
+            rims[p, 10:12, :] = sum_right[c * groups + group, span, :]
         high, low = halves(rims[...])
         for p in range(0, chunk, 2):
             result = dot(azi_use[...], stacked(high, low, p))
@@ -376,17 +409,18 @@
     x = fields.reshape(planes, cells_t, cells_r)
     chunk = 8
     count = planes // chunk
-    rims = jax.ShapeDtypeStruct((planes // PACK, PACK * EDGE, cells_r), F32)
+    raws = jax.ShapeDtypeStruct((planes, RAW, cells_r), F32)
+    sums = jax.ShapeDtypeStruct((planes // PACK, PACK * SUMS, cells_r), F32)
     full = jax.ShapeDtypeStruct(x.shape, F32)
     ends = pltpu.VMEM((2, planes * cells_t), F32)
     hbm = pl.BlockSpec(memory_space=pltpu.HBM)
     vmem = pl.BlockSpec(memory_space=pltpu.VMEM)
     dma = pltpu.SemaphoreType.DMA
-    from_left, from_right, part_slope, part_smooth, radial = pl.pallas_call(
+    raw_left, raw_right, sum_left, sum_right, part_slope, part_smooth, radial = pl.pallas_call(
         functools.partial(block_kernel, azi_count, rad_count, chunk),
-        out_shape=[rims, rims, full, full, full],
+        out_shape=[raws, raws, sums, sums, full, full, full],
         in_specs=[hbm] * 7,
-        out_specs=[vmem] * 5,
+        out_specs=[vmem] * 7,
         scratch_shapes=[
             pltpu.VMEM(x.shape, F32),
             pltpu.VMEM(azi_send.shape, BF16),
@@ -395,8 +429,8 @@
             pltpu.VMEM(rad_main.shape[1:], BF16),
             pltpu.VMEM(rad_use.shape[1:], BF16),
             pltpu.VMEM((1, cells_r), F32),
-            pltpu.VMEM(rims.shape, F32),
-            pltpu.VMEM(rims.shape, F32),
+            pltpu.VMEM(sums.shape, F32),
+            pltpu.VMEM(sums.shape, F32),
             ends,
             ends,
             ends,
@@ -404,10 +438,11 @@
             pltpu.VMEM((16, chunk * cells_t), F32),
             dma((6,)),
             dma((count,)),
-            dma((2, 1)),
-            dma((2, 1)),
+            dma((4,)),
+            dma((4,)),
             dma((2,)),
             dma((2,)),
+            pltpu.SemaphoreType.REGULAR((2,)),
         ],
         compiler_params=pltpu.CompilerParams(
             collective_id=0, has_side_effects=True, vmem_limit_bytes=24 * 2**20
@@ -422,7 +457,7 @@
     outs = pl.pallas_call(
         functools.partial(join_kernel, chunk),
         out_shape=[full] * 3,
-        in_specs=[vmem] * 7,
+        in_specs=[vmem] * 9,
         out_specs=[hbm] * 3,
         scratch_shapes=[
             pltpu.VMEM(x.shape, F32),
@@ -433,7 +468,7 @@
         ],
         compiler_params=pltpu.CompilerParams(vmem_limit_bytes=24 * 2**20),
     )(
-        part_slope, part_smooth, radial, from_left, from_right, azi_use,
+        part_slope, part_smooth, radial, raw_left, raw_right, sum_left, sum_right, azi_use,
         azimuth_metric.reshape(1, cells_r),
     )
     grad_azimuth, filtered, grad_radial = [a.reshape(shape) for a in outs]

time: 14.4 us -> 15.6 us (1.083)
  the two profiles are of different devices: /device:TPU:1 before, /device:TPU:0 now
where the time goes in v1:
time: 15.6 us; the launch traced here: 15.4 us
  Pallas kernels  14.7 us (94%)
  between operations  0.67 us (4%)
    pallas_call x1, Pallas kernels, local(): pl.pallas_call(functools.partial(block_kernel, azi_count, rad_count, chun...  12.7 us
    pallas_call x1, Pallas kernels, local(): pl.pallas_call(functools.partial(join_kernel, chunk), out_shape=[full] *...  2.01 us

profile of v1, /device:TPU:0, one launch (start us, length us, event | category | flops | bytes accessed | tf_op | source)
XLA Modules:
  0.0 15.4 jit_solution(17186660268228421116)
XLA Ops:
  0.6 0.0 copy-start
  0.6 0.0 copy-start.1
  0.7 12.7 %shard_map.112 = (f32[40,4,128]{2,1,0:T(4,128)S(1)}, f32[40,4,128]{2,1,0:T(4,128)S(1)}, f32[10,8,128]{2,1,0:T(8,128)S(1)}, f32[10,8,128]{2,1,0:T(8,128)S(1)}, f3...) custom-call(f32[40,64,128]{2,1,0:T(8,128)} %bitcast.7, ...), custom_call_target="tpu_custom_call" | custom-call | tf_op jit(solution)/shard_map/pallas_call | solution.py:419
  13.4 0.0 copy-done
  13.4 0.0 copy-done.1
  13.4 2.0 %shard_map.113 = (f32[40,64,128]{2,1,0:T(8,128)}, f32[40,64,128]{2,1,0:T(8,128)}, f32[40,64,128]{2,1,0:T(8,128)}) custom-call(f32[40,64,128]{2,1,0:T(8,128)S(1)} %get-tuple-element.13.part_slope, f32[40,64,128]{2,1,0:T(8,128)S(1)} %get-tuple-element.14.part_smooth, f32[40,64,128]{2,1,0:T(8,128)S(1)} %get-tuple-element.15.radial, ...), custom_call_target="tpu_custom_call" | custom-call | tf_op jit(solution)/shard_map/pallas_call | solution.py:457
Async XLA Ops:
  0.6 12.7 %copy-start = (bf16[128,48]{1,0:T(8,128)(2,1)S(1)}, bf16[128,48]{1,0:T(8,128)(2,1)}, u32[]{:S(2)}) copy-start(bf16[128,48]{1,0:T(8,128)(2,1)} %constant.14.clone.azi_use) | copy-start | bytes 36868
  0.6 12.7 %copy-start.1 = (f32[128]{0:T(128)S(1)}, f32[128]{0:T(128)}, u32[]{:S(2)}) copy-start(f32[128]{0:T(128)} %param.11) | copy-start | bytes 1540

commit v2 on v1

--- a/solution.py
+++ b/solution.py
@@ -176,12 +176,28 @@
     outer = (lax.rem(rad + 1, rad_count), azi)
     inner = (lax.rem(rad + rad_count - 1, rad_count), azi)
     has_outer, has_inner = rad < rad_count - 1, rad > 0
+    is_first, is_last = azi == 0, azi == azi_count - 1
+    is_second, is_third = azi == 1, azi == 2
+    early = jnp.logical_or(is_second, is_last)
+    even = lax.rem(rad, 2) == 0
+    odd = jnp.logical_not(even)
     barrier = pltpu.get_barrier_semaphore()
-    pl.semaphore_signal(barrier, inc=1, device_id=left, device_id_type=MESH)
-
-    @pl.when(has_outer)
+
+    @pl.when(jnp.logical_not(is_third))
+    def _():
+        pl.semaphore_signal(barrier, inc=1, device_id=left, device_id_type=MESH)
+
+    @pl.when(jnp.logical_not(is_last))
+    def _():
+        pl.semaphore_signal(barrier, inc=1, device_id=right, device_id_type=MESH)
+
+    @pl.when(jnp.logical_and(odd, has_outer))
     def _():
         pl.semaphore_signal(barrier, inc=1, device_id=outer, device_id_type=MESH)
+
+    @pl.when(odd)
+    def _():
+        pl.semaphore_signal(barrier, inc=1, device_id=inner, device_id_type=MESH)
 
     def load(c):
         span = pl.ds(c * chunk, chunk)
@@ -236,13 +252,54 @@
     for table in tables[1:]:
         table.start()
 
-    pl.semaphore_wait(barrier, 1 + has_inner.astype(jnp.int32))
-    raw_sends[0].start()
-    pl.semaphore_signal(ready.at[0], inc=1, device_id=right, device_id_type=MESH)
-
-    @pl.when(has_inner)
-    def _():
-        pl.semaphore_signal(ready.at[1], inc=1, device_id=inner, device_id_type=MESH)
+    def first(pair):
+        @pl.when(right_first)
+        def _():
+            pair[0].start()
+
+        @pl.when(jnp.logical_not(right_first))
+        def _():
+            pair[1].start()
+
+    def second(pair):
+        @pl.when(right_first)
+        def _():
+            pair[1].start()
+
+        @pl.when(jnp.logical_not(right_first))
+        def _():
+            pair[0].start()
+
+    def greet():
+        neighbours = jnp.where(azi < 2, 1, 2)
+        beside = has_inner.astype(jnp.int32) + has_outer.astype(jnp.int32)
+        pl.semaphore_wait(barrier, neighbours + jnp.where(even, beside, 0))
+
+        @pl.when(is_last)
+        def _():
+            pl.semaphore_signal(ready.at[0], inc=1, device_id=right, device_id_type=MESH)
+
+        @pl.when(is_third)
+        def _():
+            pl.semaphore_signal(ready.at[0], inc=1, device_id=left, device_id_type=MESH)
+
+        @pl.when(jnp.logical_and(even, has_inner))
+        def _():
+            pl.semaphore_signal(ready.at[1], inc=1, device_id=inner, device_id_type=MESH)
+
+        @pl.when(jnp.logical_and(even, has_outer))
+        def _():
+            pl.semaphore_signal(ready.at[2], inc=1, device_id=outer, device_id_type=MESH)
+
+    @pl.when(early)
+    def _():
+        greet()
+
+        @pl.when(is_last)
+        def _():
+            raw_sends[0].start()
+
+        raw_sends[1].start()
 
     tables[0].wait()
 
@@ -259,7 +316,26 @@
                 to_right[c * groups + group, span, :] = edge[0:SUMS, lanes]
                 to_left[c * groups + group, span, :] = edge[SUMS : 2 * SUMS, lanes]
 
-    sum_sends[0].start()
+    @pl.when(early)
+    def _():
+        @pl.when(is_last)
+        def _():
+            sum_sends[0].start()
+
+        sum_sends[1].start()
+
+    @pl.when(jnp.logical_not(early))
+    def _():
+        greet()
+
+        @pl.when(jnp.logical_not(is_first))
+        def _():
+            raw_sends[1].start()
+            sum_sends[1].start()
+
+        raw_sends[0].start()
+        sum_sends[0].start()
+
     tables[1].wait()
 
     @pl.loop(0, count)
@@ -276,16 +352,26 @@
 
     @pl.when(has_inner)
     def _():
+        @pl.when(odd)
+        def _():
+            pl.semaphore_wait(ready.at[2], 1)
+
         in_send.start()
 
     @pl.when(has_outer)
     def _():
-        pl.semaphore_wait(ready.at[1], 1)
+        @pl.when(odd)
+        def _():
+            pl.semaphore_wait(ready.at[1], 1)
+
         out_send.start()
 
-    pl.semaphore_wait(ready.at[0], 1)
-    raw_sends[1].start()
-    sum_sends[1].start()
+    @pl.when(is_second)
+    def _():
+        pl.semaphore_wait(ready.at[0], 1)
+        raw_sends[0].start()
+        sum_sends[0].start()
+
     for table in tables[2:]:
         table.wait()
     ends[...] = jnp.zeros_like(ends)
@@ -299,6 +385,12 @@
                 lanes = slice(k * cells_r, (k + 1) * cells_r)
                 part_slope[c * chunk + p + k] = result[:cells_t, lanes]
                 part_smooth[c * chunk + p + k] = result[cells_t:, lanes]
+
+    @pl.when(is_first)
+    def _():
+        pl.semaphore_wait(ready.at[0], 1)
+        raw_sends[1].start()
+        sum_sends[1].start()
 
     @pl.when(has_inner)
     def _():
@@ -442,7 +534,7 @@
             dma((4,)),
             dma((2,)),
             dma((2,)),
-            pltpu.SemaphoreType.REGULAR((2,)),
+            pltpu.SemaphoreType.REGULAR((3,)),
         ],
         compiler_params=pltpu.CompilerParams(
             collective_id=0, has_side_effects=True, vmem_limit_bytes=24 * 2**20

time: 15.6 us -> 13.1 us (0.84)
  Pallas kernels: 14.7 us -> 12.3 us
    pallas_call x1, Pallas kernels: 12.7 us -> 10.3 us  [local(): pl.pallas_call(functools.partial(block_kernel, azi_count, rad_count, chun...]
where the time goes in v2:
time: 13.1 us; the launch traced here: 13 us
  Pallas kernels  12.3 us (94%)
  between operations  0.67 us (5%)
    pallas_call x1, Pallas kernels, local(): pl.pallas_call(functools.partial(block_kernel, azi_count, rad_count, chun...  10.3 us
    pallas_call x1, Pallas kernels, local(): pl.pallas_call(functools.partial(join_kernel, chunk), out_shape=[full] *...  2.01 us

profile of v2, /device:TPU:0, one launch (start us, length us, event | category | flops | bytes accessed | tf_op | source)
XLA Modules:
  0.0 13.0 jit_solution(10852238697128116946)
XLA Ops:
  0.6 0.0 copy-start
  0.6 0.0 copy-start.1
  0.7 10.3 %shard_map.112 = (f32[40,4,128]{2,1,0:T(4,128)S(1)}, f32[40,4,128]{2,1,0:T(4,128)S(1)}, f32[10,8,128]{2,1,0:T(8,128)S(1)}, f32[10,8,128]{2,1,0:T(8,128)S(1)}, f3...) custom-call(f32[40,64,128]{2,1,0:T(8,128)} %bitcast.7, ...), custom_call_target="tpu_custom_call" | custom-call | tf_op jit(solution)/shard_map/pallas_call | solution.py:511
  11.0 0.0 copy-done
  11.0 0.0 copy-done.1
  11.0 2.0 %shard_map.113 = (f32[40,64,128]{2,1,0:T(8,128)}, f32[40,64,128]{2,1,0:T(8,128)}, f32[40,64,128]{2,1,0:T(8,128)}) custom-call(f32[40,64,128]{2,1,0:T(8,128)S(1)} %get-tuple-element.13.part_slope, f32[40,64,128]{2,1,0:T(8,128)S(1)} %get-tuple-element.14.part_smooth, f32[40,64,128]{2,1,0:T(8,128)S(1)} %get-tuple-element.15.radial, ...), custom_call_target="tpu_custom_call" | custom-call | tf_op jit(solution)/shard_map/pallas_call | solution.py:549
Async XLA Ops:
  0.6 10.3 %copy-start = (bf16[128,48]{1,0:T(8,128)(2,1)S(1)}, bf16[128,48]{1,0:T(8,128)(2,1)}, u32[]{:S(2)}) copy-start(bf16[128,48]{1,0:T(8,128)(2,1)} %constant.14.clone.azi_use) | copy-start | bytes 36868
  0.6 10.3 %copy-start.1 = (f32[128]{0:T(128)S(1)}, f32[128]{0:T(128)}, u32[]{:S(2)}) copy-start(f32[128]{0:T(128)} %param.11) | copy-start | bytes 1540

commit v3 on v2

--- a/solution.py
+++ b/solution.py
@@ -177,17 +177,19 @@
     inner = (lax.rem(rad + rad_count - 1, rad_count), azi)
     has_outer, has_inner = rad < rad_count - 1, rad > 0
     is_first, is_last = azi == 0, azi == azi_count - 1
-    is_second, is_third = azi == 1, azi == 2
-    early = jnp.logical_or(is_second, is_last)
+    last = azi_count - 1
+    early = jnp.logical_and(lax.rem(azi, 2) == 1, azi != last - 2)
+    tells_left = jnp.logical_and(lax.rem(azi, 2) == 0, jnp.logical_and(azi > 0, azi < last - 1))
+    late = jnp.logical_not(early)
     even = lax.rem(rad, 2) == 0
     odd = jnp.logical_not(even)
     barrier = pltpu.get_barrier_semaphore()
 
-    @pl.when(jnp.logical_not(is_third))
+    @pl.when(jnp.logical_not(tells_left))
     def _():
         pl.semaphore_signal(barrier, inc=1, device_id=left, device_id_type=MESH)
 
-    @pl.when(jnp.logical_not(is_last))
+    @pl.when(azi < azi_count - 2)
     def _():
         pl.semaphore_signal(barrier, inc=1, device_id=right, device_id_type=MESH)
 
@@ -231,7 +233,16 @@
         send(0, fields.at[:, pl.ds(cells_t - RAW, RAW)], raw_left, right),
         send(1, fields.at[:, pl.ds(0, RAW)], raw_right, left),
     )
-    sum_sends = (send(2, to_right, sum_left, right), send(3, to_left, sum_right, left))
+    cuts = [0, count - 2, count]
+
+    def sums(part):
+        span = pl.ds(cuts[part] * groups, (cuts[part + 1] - cuts[part]) * groups)
+        return (
+            send(2 + 2 * part, to_right.at[span], sum_left.at[span], right),
+            send(3 + 2 * part, to_left.at[span], sum_right.at[span], left),
+        )
+
+    sum_sends = [sums(part) for part in range(len(cuts) - 1)]
     out_send, in_send = [
         pltpu.make_async_remote_copy(
             src_ref=source,
@@ -270,16 +281,34 @@
         def _():
             pair[0].start()
 
+    def early_first(pair):
+        @pl.when(is_last)
+        def _():
+            pair[0].start()
+
+        @pl.when(jnp.logical_and(early, jnp.logical_not(is_last)))
+        def _():
+            pair[1].start()
+
+    def early_second(pair):
+        @pl.when(is_last)
+        def _():
+            pair[1].start()
+
+        @pl.when(jnp.logical_and(early, jnp.logical_not(is_last)))
+        def _():
+            pair[0].start()
+
     def greet():
-        neighbours = jnp.where(azi < 2, 1, 2)
+        neighbours = jnp.where(jnp.logical_or(early, is_first), 1, 2)
         beside = has_inner.astype(jnp.int32) + has_outer.astype(jnp.int32)
         pl.semaphore_wait(barrier, neighbours + jnp.where(even, beside, 0))
 
-        @pl.when(is_last)
+        @pl.when(azi >= azi_count - 2)
         def _():
             pl.semaphore_signal(ready.at[0], inc=1, device_id=right, device_id_type=MESH)
 
-        @pl.when(is_third)
+        @pl.when(tells_left)
         def _():
             pl.semaphore_signal(ready.at[0], inc=1, device_id=left, device_id_type=MESH)
 
@@ -295,16 +324,10 @@
     def _():
         greet()
 
-        @pl.when(is_last)
-        def _():
-            raw_sends[0].start()
-
-        raw_sends[1].start()
-
+    early_first(raw_sends)
     tables[0].wait()
 
-    @pl.loop(0, count)
-    def _(c):
+    def edges(c):
         load(c).wait()
         high, low = halves(block[pl.ds(c * chunk, chunk)])
         for p in range(0, chunk, 2):
@@ -316,25 +339,23 @@
                 to_right[c * groups + group, span, :] = edge[0:SUMS, lanes]
                 to_left[c * groups + group, span, :] = edge[SUMS : 2 * SUMS, lanes]
 
-    @pl.when(early)
-    def _():
-        @pl.when(is_last)
-        def _():
-            sum_sends[0].start()
-
-        sum_sends[1].start()
-
-    @pl.when(jnp.logical_not(early))
+    for part in range(len(cuts) - 1):
+        pl.loop(cuts[part], cuts[part + 1])(edges)
+        early_first(sum_sends[part])
+
+    @pl.when(late)
     def _():
         greet()
 
         @pl.when(jnp.logical_not(is_first))
         def _():
             raw_sends[1].start()
-            sum_sends[1].start()
+            for pair in sum_sends:
+                pair[1].start()
 
         raw_sends[0].start()
-        sum_sends[0].start()
+        for pair in sum_sends:
+            pair[0].start()
 
     tables[1].wait()
 
@@ -366,11 +387,13 @@
 
         out_send.start()
 
-    @pl.when(is_second)
+    @pl.when(early)
     def _():
         pl.semaphore_wait(ready.at[0], 1)
-        raw_sends[0].start()
-        sum_sends[0].start()
+
+    early_second(raw_sends)
+    for pair in sum_sends:
+        early_second(pair)
 
     for table in tables[2:]:
         table.wait()
@@ -390,7 +413,8 @@
     def _():
         pl.semaphore_wait(ready.at[0], 1)
         raw_sends[1].start()
-        sum_sends[1].start()
+        for pair in sum_sends:
+            pair[1].start()
 
     @pl.when(has_inner)
     def _():
@@ -429,8 +453,9 @@
         slope = (both[:, :cells_r] + both[:, cells_r:] + outside) * metric[...]
         grad_radial[pl.ds(c * chunk, chunk)] = slope.reshape(chunk, cells_t, cells_r)
 
-    for copy in raw_sends + sum_sends:
-        copy.wait()
+    for pair in [raw_sends] + sum_sends:
+        for copy in pair:
+            copy.wait()
 
 
 def stacked(high, low, p):
@@ -530,8 +555,8 @@
             pltpu.VMEM((16, chunk * cells_t), F32),
             dma((6,)),
             dma((count,)),
-            dma((4,)),
-            dma((4,)),
+            dma((8,)),
+            dma((8,)),
             dma((2,)),
             dma((2,)),
             pltpu.SemaphoreType.REGULAR((3,)),

time: 13.1 us -> 12.8 us (0.977)
  Pallas kernels: 12.3 us -> 12 us
    pallas_call x1, Pallas kernels: 10.3 us -> 9.96 us  [local(): pl.pallas_call(functools.partial(block_kernel, azi_count, rad_count, chun...]
where the time goes in v3:
time: 12.8 us; the launch traced here: 12.6 us
  Pallas kernels  12 us (94%)
  between operations  0.67 us (5%)
    pallas_call x1, Pallas kernels, local(): pl.pallas_call(functools.partial(block_kernel, azi_count, rad_count, chun...  9.96 us
    pallas_call x1, Pallas kernels, local(): pl.pallas_call(functools.partial(join_kernel, chunk), out_shape=[full] *...  2.01 us

profile of v3, /device:TPU:0, one launch (start us, length us, event | category | flops | bytes accessed | tf_op | source)
XLA Modules:
  0.0 12.6 jit_solution(13324165509226444580)
XLA Ops:
  0.6 0.0 copy-start
  0.6 0.0 copy-start.1
  0.7 10.0 %shard_map.112 = (f32[40,4,128]{2,1,0:T(4,128)S(1)}, f32[40,4,128]{2,1,0:T(4,128)S(1)}, f32[10,8,128]{2,1,0:T(8,128)S(1)}, f32[10,8,128]{2,1,0:T(8,128)S(1)}, f3...) custom-call(f32[40,64,128]{2,1,0:T(8,128)} %bitcast.7, ...), custom_call_target="tpu_custom_call" | custom-call | tf_op jit(solution)/shard_map/pallas_call | solution.py:536
  10.6 0.0 copy-done
  10.6 0.0 copy-done.1
  10.6 2.0 %shard_map.113 = (f32[40,64,128]{2,1,0:T(8,128)}, f32[40,64,128]{2,1,0:T(8,128)}, f32[40,64,128]{2,1,0:T(8,128)}) custom-call(f32[40,64,128]{2,1,0:T(8,128)S(1)} %get-tuple-element.13.part_slope, f32[40,64,128]{2,1,0:T(8,128)S(1)} %get-tuple-element.14.part_smooth, f32[40,64,128]{2,1,0:T(8,128)S(1)} %get-tuple-element.15.radial, ...), custom_call_target="tpu_custom_call" | custom-call | tf_op jit(solution)/shard_map/pallas_call | solution.py:574
Async XLA Ops:
  0.6 10.0 %copy-start = (bf16[128,48]{1,0:T(8,128)(2,1)S(1)}, bf16[128,48]{1,0:T(8,128)(2,1)}, u32[]{:S(2)}) copy-start(bf16[128,48]{1,0:T(8,128)(2,1)} %constant.14.clone.azi_use) | copy-start | bytes 36868
  0.6 10.0 %copy-start.1 = (f32[128]{0:T(128)S(1)}, f32[128]{0:T(128)}, u32[]{:S(2)}) copy-start(f32[128]{0:T(128)} %param.11) | copy-start | bytes 1540

commit v4 on v3

--- a/solution.py
+++ b/solution.py
@@ -118,10 +118,8 @@
 
 def build_tables(cells_t, azi_count, cells_r, rad_count):
     main, edge_sums, edge_uses = azimuth_tables(cells_t, azi_count)
-    sends = np.zeros((16, cells_t))
-    sends[: 2 * SUMS] = edge_sums
-    high, low = split(sends)
-    azi_send = np.concatenate([high, low, high], axis=1)
+    azi_send = np.broadcast_to(edge_sums[:, :, None], edge_sums.shape + (cells_r,))
+    azi_send = np.ascontiguousarray(azi_send, np.float32)
     uses = np.zeros((2 * cells_t, 16))
     uses[:, : edge_uses.shape[1]] = edge_uses
     high, low = split(main)
@@ -329,15 +327,15 @@
 
     def edges(c):
         load(c).wait()
-        high, low = halves(block[pl.ds(c * chunk, chunk)])
-        for p in range(0, chunk, 2):
-            edge = dot(azi_send_v[...], stacked(high, low, p))
-            for k in range(2):
-                group, slot = divmod(p + k, PACK)
-                lanes = slice(k * cells_r, (k + 1) * cells_r)
-                span = slice(SUMS * slot, SUMS * (slot + 1))
-                to_right[c * groups + group, span, :] = edge[0:SUMS, lanes]
-                to_left[c * groups + group, span, :] = edge[SUMS : 2 * SUMS, lanes]
+        for p in range(chunk):
+            plane = block[c * chunk + p]
+            group, slot = divmod(p, PACK)
+            span = slice(SUMS * slot, SUMS * (slot + 1))
+            both = [
+                jnp.sum(plane * azi_send_v[k], axis=0, keepdims=True) for k in range(2 * SUMS)
+            ]
+            to_right[c * groups + group, span, :] = jnp.concatenate(both[:SUMS], axis=0)
+            to_left[c * groups + group, span, :] = jnp.concatenate(both[SUMS:], axis=0)
 
     for part in range(len(cuts) - 1):
         pl.loop(cuts[part], cuts[part + 1])(edges)
@@ -371,20 +369,12 @@
         to_out[:, span] = tips[0:2]
         to_in[:, span] = tips[2:4]
 
-    @pl.when(has_inner)
-    def _():
-        @pl.when(odd)
-        def _():
-            pl.semaphore_wait(ready.at[2], 1)
-
+    @pl.when(jnp.logical_and(even, has_inner))
+    def _():
         in_send.start()
 
-    @pl.when(has_outer)
-    def _():
-        @pl.when(odd)
-        def _():
-            pl.semaphore_wait(ready.at[1], 1)
-
+    @pl.when(jnp.logical_and(even, has_outer))
+    def _():
         out_send.start()
 
     @pl.when(early)
@@ -415,6 +405,16 @@
         raw_sends[1].start()
         for pair in sum_sends:
             pair[1].start()
+
+    @pl.when(odd)
+    def _():
+        pl.semaphore_wait(ready.at[2], 1)
+        in_send.start()
+
+    @pl.when(jnp.logical_and(odd, has_outer))
+    def _():
+        pl.semaphore_wait(ready.at[1], 1)
+        out_send.start()
 
     @pl.when(has_inner)
     def _():
@@ -540,7 +540,7 @@
         out_specs=[vmem] * 7,
         scratch_shapes=[
             pltpu.VMEM(x.shape, F32),
-            pltpu.VMEM(azi_send.shape, BF16),
+            pltpu.VMEM(azi_send.shape, F32),
             pltpu.VMEM(azi_main.shape, BF16),
             pltpu.VMEM(rad_send.shape[1:], BF16),
             pltpu.VMEM(rad_main.shape[1:], BF16),

time: 12.8 us -> 12.8 us (level)
  no operation moved by 1% of the time
where the time goes in v4:
time: 12.8 us; the launch traced here: 12.6 us
  Pallas kernels  11.9 us (93%)
  between operations  0.67 us (5%)
    pallas_call x1, Pallas kernels, local(): pl.pallas_call(functools.partial(block_kernel, azi_count, rad_count, chun...  9.93 us
    pallas_call x1, Pallas kernels, local(): pl.pallas_call(functools.partial(join_kernel, chunk), out_shape=[full] *...  2.01 us

profile of v4, /device:TPU:0, one launch (start us, length us, event | category | flops | bytes accessed | tf_op | source)
XLA Modules:
  0.0 12.6 jit_solution(11198445190791518497)
XLA Ops:
  0.6 0.0 copy-start
  0.6 0.0 copy-start.1
  0.7 9.9 %shard_map.112 = (f32[40,4,128]{2,1,0:T(4,128)S(1)}, f32[40,4,128]{2,1,0:T(4,128)S(1)}, f32[10,8,128]{2,1,0:T(8,128)S(1)}, f32[10,8,128]{2,1,0:T(8,128)S(1)}, f3...) custom-call(f32[40,64,128]{2,1,0:T(8,128)} %bitcast.7, ...), custom_call_target="tpu_custom_call" | custom-call | tf_op jit(solution)/shard_map/pallas_call | solution.py:536
  10.6 0.0 copy-done
  10.6 0.0 copy-done.1
  10.6 2.0 %shard_map.113 = (f32[40,64,128]{2,1,0:T(8,128)}, f32[40,64,128]{2,1,0:T(8,128)}, f32[40,64,128]{2,1,0:T(8,128)}) custom-call(f32[40,64,128]{2,1,0:T(8,128)S(1)} %get-tuple-element.13.part_slope, f32[40,64,128]{2,1,0:T(8,128)S(1)} %get-tuple-element.14.part_smooth, f32[40,64,128]{2,1,0:T(8,128)S(1)} %get-tuple-element.15.radial, ...), custom_call_target="tpu_custom_call" | custom-call | tf_op jit(solution)/shard_map/pallas_call | solution.py:574
Async XLA Ops:
  0.6 10.0 %copy-start = (bf16[128,48]{1,0:T(8,128)(2,1)S(1)}, bf16[128,48]{1,0:T(8,128)(2,1)}, u32[]{:S(2)}) copy-start(bf16[128,48]{1,0:T(8,128)(2,1)} %constant.14.clone.azi_use) | copy-start | bytes 36868
  0.6 10.0 %copy-start.1 = (f32[128]{0:T(128)S(1)}, f32[128]{0:T(128)}, u32[]{:S(2)}) copy-start(f32[128]{0:T(128)} %param.11) | copy-start | bytes 1540

commit v5 on v4

--- a/solution.py
+++ b/solution.py
@@ -231,7 +231,7 @@
         send(0, fields.at[:, pl.ds(cells_t - RAW, RAW)], raw_left, right),
         send(1, fields.at[:, pl.ds(0, RAW)], raw_right, left),
     )
-    cuts = [0, count - 2, count]
+    cuts = [0, count - 1, count]
 
     def sums(part):
         span = pl.ds(cuts[part] * groups, (cuts[part + 1] - cuts[part]) * groups)
@@ -255,74 +255,79 @@
         )
     ]
 
+    def first(pair):
+        @pl.when(right_first)
+        def _():
+            pair[0].start()
+
+        @pl.when(jnp.logical_not(right_first))
+        def _():
+            pair[1].start()
+
+    def second(pair):
+        @pl.when(right_first)
+        def _():
+            pair[1].start()
+
+        @pl.when(jnp.logical_not(right_first))
+        def _():
+            pair[0].start()
+
+    def early_first(pair):
+        @pl.when(is_last)
+        def _():
+            pair[0].start()
+
+        @pl.when(jnp.logical_and(early, jnp.logical_not(is_last)))
+        def _():
+            pair[1].start()
+
+    def early_second(pair):
+        @pl.when(is_last)
+        def _():
+            pair[1].start()
+
+        @pl.when(jnp.logical_and(early, jnp.logical_not(is_last)))
+        def _():
+            pair[0].start()
+
+    def greet():
+        neighbours = jnp.where(jnp.logical_or(early, is_first), 1, 2)
+        beside = has_inner.astype(jnp.int32) + has_outer.astype(jnp.int32)
+        pl.semaphore_wait(barrier, neighbours + jnp.where(even, beside, 0))
+
+        @pl.when(azi >= azi_count - 2)
+        def _():
+            pl.semaphore_signal(ready.at[0], inc=1, device_id=right, device_id_type=MESH)
+
+        @pl.when(tells_left)
+        def _():
+            pl.semaphore_signal(ready.at[0], inc=1, device_id=left, device_id_type=MESH)
+
+        @pl.when(jnp.logical_and(even, has_inner))
+        def _():
+            pl.semaphore_signal(ready.at[1], inc=1, device_id=inner, device_id_type=MESH)
+
+        @pl.when(jnp.logical_and(even, has_outer))
+        def _():
+            pl.semaphore_signal(ready.at[2], inc=1, device_id=outer, device_id_type=MESH)
+
+    @pl.when(is_last)
+    def _():
+        greet()
+        raw_sends[0].start()
+
     tables[0].start()
     for c in range(count):
         load(c).start()
     for table in tables[1:]:
         table.start()
 
-    def first(pair):
-        @pl.when(right_first)
-        def _():
-            pair[0].start()
-
-        @pl.when(jnp.logical_not(right_first))
-        def _():
-            pair[1].start()
-
-    def second(pair):
-        @pl.when(right_first)
-        def _():
-            pair[1].start()
-
-        @pl.when(jnp.logical_not(right_first))
-        def _():
-            pair[0].start()
-
-    def early_first(pair):
-        @pl.when(is_last)
-        def _():
-            pair[0].start()
-
-        @pl.when(jnp.logical_and(early, jnp.logical_not(is_last)))
-        def _():
-            pair[1].start()
-
-    def early_second(pair):
-        @pl.when(is_last)
-        def _():
-            pair[1].start()
-
-        @pl.when(jnp.logical_and(early, jnp.logical_not(is_last)))
-        def _():
-            pair[0].start()
-
-    def greet():
-        neighbours = jnp.where(jnp.logical_or(early, is_first), 1, 2)
-        beside = has_inner.astype(jnp.int32) + has_outer.astype(jnp.int32)
-        pl.semaphore_wait(barrier, neighbours + jnp.where(even, beside, 0))
-
-        @pl.when(azi >= azi_count - 2)
-        def _():
-            pl.semaphore_signal(ready.at[0], inc=1, device_id=right, device_id_type=MESH)
-
-        @pl.when(tells_left)
-        def _():
-            pl.semaphore_signal(ready.at[0], inc=1, device_id=left, device_id_type=MESH)
-
-        @pl.when(jnp.logical_and(even, has_inner))
-        def _():
-            pl.semaphore_signal(ready.at[1], inc=1, device_id=inner, device_id_type=MESH)
-
-        @pl.when(jnp.logical_and(even, has_outer))
-        def _():
-            pl.semaphore_signal(ready.at[2], inc=1, device_id=outer, device_id_type=MESH)
-
-    @pl.when(early)
+    @pl.when(jnp.logical_and(early, jnp.logical_not(is_last)))
     def _():
         greet()
-
-    early_first(raw_sends)
+        raw_sends[1].start()
+
     tables[0].wait()
 
     def edges(c):

time: 12.8 us -> 12.8 us (level)
  no operation moved by 1% of the time
where the time goes in v5:
time: 12.8 us; the launch traced here: 12.6 us
  Pallas kernels  11.9 us (93%)
  between operations  0.67 us (5%)
    pallas_call x1, Pallas kernels, local(): pl.pallas_call(functools.partial(block_kernel, azi_count, rad_count, chun...  9.92 us
    pallas_call x1, Pallas kernels, local(): pl.pallas_call(functools.partial(join_kernel, chunk), out_shape=[full] *...  2.01 us

profile of v5, /device:TPU:0, one launch (start us, length us, event | category | flops | bytes accessed | tf_op | source)
XLA Modules:
  0.0 12.6 jit_solution(16711816572913135680)
XLA Ops:
  0.6 0.0 copy-start
  0.6 0.0 copy-start.1
  0.7 9.9 %shard_map.112 = (f32[40,4,128]{2,1,0:T(4,128)S(1)}, f32[40,4,128]{2,1,0:T(4,128)S(1)}, f32[10,8,128]{2,1,0:T(8,128)S(1)}, f32[10,8,128]{2,1,0:T(8,128)S(1)}, f3...) custom-call(f32[40,64,128]{2,1,0:T(8,128)} %bitcast.7, ...), custom_call_target="tpu_custom_call" | custom-call | tf_op jit(solution)/shard_map/pallas_call | solution.py:541
  10.6 0.0 copy-done
  10.6 0.0 copy-done.1
  10.6 2.0 %shard_map.113 = (f32[40,64,128]{2,1,0:T(8,128)}, f32[40,64,128]{2,1,0:T(8,128)}, f32[40,64,128]{2,1,0:T(8,128)}) custom-call(f32[40,64,128]{2,1,0:T(8,128)S(1)} %get-tuple-element.13.part_slope, f32[40,64,128]{2,1,0:T(8,128)S(1)} %get-tuple-element.14.part_smooth, f32[40,64,128]{2,1,0:T(8,128)S(1)} %get-tuple-element.15.radial, ...), custom_call_target="tpu_custom_call" | custom-call | tf_op jit(solution)/shard_map/pallas_call | solution.py:579
Async XLA Ops:
  0.6 10.0 %copy-start = (bf16[128,48]{1,0:T(8,128)(2,1)S(1)}, bf16[128,48]{1,0:T(8,128)(2,1)}, u32[]{:S(2)}) copy-start(bf16[128,48]{1,0:T(8,128)(2,1)} %constant.14.clone.azi_use) | copy-start | bytes 36868
  0.6 10.0 %copy-start.1 = (f32[128]{0:T(128)S(1)}, f32[128]{0:T(128)}, u32[]{:S(2)}) copy-start(f32[128]{0:T(128)} %param.11) | copy-start | bytes 1540
